TPU v7x, 256 devices: a whole 4x4x8 slice. The times are simulated.
256 devices in a mesh: bkt: 32 (over y, z_lo, x), grp: 8 (over z_hi, core).
Axes of the slice: x: 4, y: 4, z: 8 (z_hi: 4, z_lo: 2; z = z_hi * 2 + z_lo), core: 2. Of those that a mesh axis runs over, the one named last changes fastest.
Arguments:
- record_tiles: bfloat16 [49152, 128, 128], P(('bkt', 'grp')), may hold values from 0.0019989014 to 0.049804688
- tile_row: int32 [49152], P(('bkt', 'grp')), may hold values from -1 to 63, as said below
- tile_col: int32 [49152], P(('bkt', 'grp')), may hold values from -1 to 255, as said below
- move_blocks: int32 [256, 64], P('bkt', 'grp'), may hold values 0 or 1
- pairing: int32 [256], replicated, may hold values from 0 to 255, as said below
Outputs:
- updated_panel: float32 [256, 32768], P('bkt', 'grp')
- gains: float32 [256, 64, 128], P('bkt', 'grp')
Inputs may be any that keep to these rules, and one draw needn't show every extreme that they name: On each device the live slots come first and no pair (tile_row, tile_col) appears twice; a device has 192, 96, 48 or 24 live slots, and some device has all 192; an empty slot has -1 here and in tile_col. `tile_col`: -1 exactly where tile_row is -1. `pairing`: an involution without fixed points. With owner(b) = b // 8, bucket b pairs with a bucket of the same position b % 8 within its owner, and the 8 buckets of one owner pair with buckets of 8 different owners.
All inputs are finite; a program needn't handle non-finite values. No bound on the sum of `move_blocks` on one device may be relied on, other than what follows from the above.
Results may differ from a plain program's by a relative error of at most 0.0003.
Values may be sent and summed in bfloat16 or wider, within the bound.
A program may use at most 64 MiB of HBM per device.

v0:
```python
import jax
import jax.numpy as jnp
from jax import lax
from jax.sharding import PartitionSpec as P

BPO = 8
TILE = 128
RTG = 8
QT = 256


survival_rate = 0.5
highest = lax.Precision.HIGHEST


def tile_terms(record_tiles, panels, segment):
    looked = jnp.take(panels.reshape(panels.shape[0], BPO * QT, TILE), segment, axis=1)
    return jnp.einsum("krq,jkq->jkr", record_tiles, looked, preferred_element_type=jnp.float32)


def local(record_tiles, tile_row, tile_col, move_blocks, pairing):
    live_mask = tile_row >= 0
    live_float = live_mask.astype(jnp.float32)
    row_index = jnp.where(live_mask, tile_row, 0)
    col_index = jnp.where(live_mask, tile_col, 0)
    segment = row_index // RTG * QT + col_index
    moving = jnp.take(move_blocks.reshape(BPO * RTG), row_index).astype(jnp.float32) * live_float
    column_sums = jnp.sum(record_tiles, axis=1, dtype=jnp.float32)
    weighted = jnp.stack([column_sums * live_float[:, None], column_sums * moving[:, None]])
    seg_table = ((jnp.arange(BPO * QT)[:, None] == segment[None, :]) & live_mask[None, :]).astype(
        jnp.float32
    )
    summed = jnp.einsum("sk,jkq->jsq", seg_table, weighted, precision=highest).reshape(
        2, BPO, QT * TILE
    )
    counts, deltas = (
        lax.psum_scatter(summed[0], "grp", scatter_dimension=1, tiled=True),
        lax.psum_scatter(summed[1], "grp", scatter_dimension=1, tiled=True),
    )
    panel_own = jnp.exp(-survival_rate * counts).astype(jnp.bfloat16)
    record_table = (
        (jnp.arange(BPO * RTG)[:, None] == row_index[None, :]) & live_mask[None, :]
    ).astype(jnp.float32)
    partner_own = lax.dynamic_slice_in_dim(pairing, lax.axis_index("bkt") * BPO, BPO)
    pieces = (
        lax.all_gather(counts, "bkt", axis=0, tiled=True),
        lax.all_gather(deltas, "bkt", axis=0, tiled=True),
    )
    local_pick = (partner_own[:, None] == jnp.arange(pieces[0].shape[0])[None, :]).astype(
        jnp.float32
    )
    first = jnp.dot(local_pick, pieces[0], precision=highest, preferred_element_type=jnp.float32)
    second = jnp.dot(local_pick, pieces[1], precision=highest, preferred_element_type=jnp.float32)
    partner16 = jnp.exp(-survival_rate * first).astype(jnp.bfloat16)
    updated_panel = jnp.exp(-survival_rate * (counts - deltas + second))
    own_wide, partner_wide = (
        lax.all_gather(panel_own, "grp", axis=1, tiled=True),
        lax.all_gather(partner16, "grp", axis=1, tiled=True),
    )
    both_sums = jnp.einsum(
        "rk,jkq->jrq",
        record_table,
        tile_terms(record_tiles, jnp.stack([own_wide, partner_wide]), segment),
        precision=highest,
    )
    own_sum = both_sums[0]
    other_sum = both_sums[1]
    gains = (survival_rate * (own_sum - other_sum)).reshape(BPO, RTG, TILE)
    return (updated_panel, gains)


def solution(mesh):
    placed = (
        P(("bkt", "grp"), None, None),
        P(("bkt", "grp")),
        P(("bkt", "grp")),
        P("bkt", "grp"),
        P(),
    )
    return jax.shard_map(
        local,
        mesh=mesh,
        in_specs=placed,
        out_specs=(P("bkt", "grp"), P("bkt", "grp", None)),
        check_vma=False,
    )
```

profile of v0, /device:TPU:2, one launch (start us, length us, event | category | flops | bytes accessed | tf_op | source)
XLA Modules:
  0.0 433.0 jit_solution(9354954340662141519)
XLA Ops:
  7.2 0.0 reduce-scatter.3.cloned.1.call-start
  7.2 0.7 compare_and_fusion
  7.9 0.8 reshape.87
  8.7 1.6 gather_fusion
  10.3 5.0 %convert_reduce_fusion = f32[192,128]{1,0:T(8,128)S(1)} fusion(bf16[192,128,128]{2,1,0:T(8,128)(2,1)} %param.5), kind=kLoop, calls=%fused_computation.2 | loop fusion | flops 6266880 | bytes 6389760 | tf_op jit(solution)/shard_map/reduce_sum | solution.py:28
  15.3 0.1 bitcast_multiply_fusion.1
  15.4 1.2 convolution_bitcast_fusion
  16.6 0.2 fusion.30
  16.8 0.3 copy.7
  17.2 1.2 squeeze.8
  18.4 0.0 reduce-scatter.5.cloned.1.call-start
  18.5 0.3 copy.8
  18.8 1.2 squeeze.9
  20.0 0.0 all-gather.5.cloned.1.call-start
  20.0 40.8 %reduce-scatter.3.cloned.1.call-done = f32[8,4096]{1,0:T(8,128)} async-done(((f32[8,32768]{1,0:T(8,128)}), f32[8,4096]{1,0:T(8,128)}) %reduce-scatter.3.cloned.1.call-update) | async-done | bytes 131088 | tf_op jit(solution)/shard_map/reduce_scatter | solution.py:37
  60.8 0.0 all-gather.3.cloned.1.call-start
  60.9 40.2 %reduce-scatter.5.cloned.1.call-done = f32[8,4096]{1,0:T(8,128)} async-done(((f32[8,32768]{1,0:T(8,128)}), f32[8,4096]{1,0:T(8,128)}) %reduce-scatter.5.cloned.1.call-update) | async-done | bytes 131088 | tf_op jit(solution)/shard_map/reduce_scatter | solution.py:38
  101.1 0.1 dynamic_slice.3
  101.2 0.9 exponential_convert_fusion
  102.2 15.2 %all_gather.13 = bf16[8,32768]{1,0:T(8,128)(2,1)S(1)} all-gather(bf16[8,4096]{1,0:T(8,128)(2,1)S(1)} %exponential_convert_fusion), channel_id=1, replica_groups=mesh['bkt'=32,'grp'=8] {'grp'}, dimensions={1}, use_global_device_ids=true | all-gather | bytes 589824 | tf_op jit(solution)/shard_map/all_gather | solution.py:57
  117.4 0.8 stack.18
  118.2 143.4 %all-gather.5.cloned.1.call-done = f32[256,4096]{1,0:T(8,128)} async-done(((f32[8,4096]{1,0:T(8,128)}), f32[256,4096]{1,0:T(8,128)}) %all-gather.5.cloned.1.call-update) | async-done | bytes 4194320 | tf_op jit(solution)/shard_map/all_gather | solution.py:46
  261.6 3.6 fusion.3
  265.2 15.7 %all_gather.15 = bf16[8,32768]{1,0:T(8,128)(2,1)S(1)} all-gather(bf16[8,4096]{1,0:T(8,128)(2,1)S(1)} %fusion.3), channel_id=1, replica_groups=mesh['bkt'=32,'grp'=8] {'grp'}, dimensions={1}, use_global_device_ids=true | all-gather | bytes 589824 | tf_op jit(solution)/shard_map/all_gather | solution.py:58
  280.9 0.8 stack.19
  281.7 2.4 pad_maximum_fusion
  284.1 0.8 gather_fusion.1
  285.0 6.2 %fusion.14 = f32[192,2,128]{2,1,0:T(2,128)S(1)} fusion(bf16[192,128,128]{2,1,0:T(8,128)(2,1)} %param.5, bf16[192,2,128]{2,1,0:T(2,128)(2,1)S(1)} %gather_fusion.1, pred[192]{0:T(512)(128)(4,1)S(1)} %get-tuple-element.2), kind=kOutput, calls=%fused_computation.24 | convolution fusion | flops 12632064 | bytes 6586560 | tf_op jit(solution)/shard_map/krq,jkq->jkr/dot_general | solution.py:18
  291.2 0.2 convolution_bitcast_fusion.1
  291.4 0.6 fusion.21
  292.0 130.2 %all-gather.3.cloned.1.call-done = f32[256,4096]{1,0:T(8,128)} async-done(((f32[8,4096]{1,0:T(8,128)}), f32[256,4096]{1,0:T(8,128)}) %all-gather.3.cloned.1.call-update) | async-done | bytes 4194320 | tf_op jit(solution)/shard_map/all_gather | solution.py:47
  422.2 4.3 fusion.2
  (16 shorter events, 0.1 us)
Async XLA Ops:
  7.2 53.6 %reduce-scatter.3.cloned.1.call-start = ((), (), s32[]{:S(2)}) async-start(), calls=%async_computation.2 | async-start | bytes 1179648 | tf_op jit(solution)/shard_map/reduce_scatter | solution.py:37
  17.2 83.9 %copy-start.2 = (s32[256]{0:T(256)S(1)}, s32[256]{0:T(256)}, u32[]{:S(2)}) copy-start(s32[256]{0:T(256)} %param.9) | copy-start | bytes 3076
  18.4 82.7 %reduce-scatter.5.cloned.1.call-start = ((), (), s32[]{:S(2)}) async-start(), calls=%async_computation.3 | async-start | bytes 1179648 | tf_op jit(solution)/shard_map/reduce_scatter | solution.py:38
  20.0 241.6 %all-gather.5.cloned.1.call-start = ((), (), s32[]{:S(2)}) async-start(), calls=%async_computation.5 | async-start | bytes 4325376 | tf_op jit(solution)/shard_map/all_gather | solution.py:46
  60.8 361.4 %all-gather.3.cloned.1.call-start = ((), (), s32[]{:S(2)}) async-start(), calls=%async_computation.4 | async-start | bytes 4325376 | tf_op jit(solution)/shard_map/all_gather | solution.py:47
  284.1 138.1 %copy-start = (f32[8,4096]{1,0:T(8,128)S(1)}, f32[8,4096]{1,0:T(8,128)}, u32[]{:S(2)}) copy-start(f32[8,4096]{1,0:T(8,128)} %reduce-scatter.3.cloned.1.call-done) | copy-start | bytes 393220
  284.1 138.1 %copy-start.1 = (f32[8,4096]{1,0:T(8,128)S(1)}, f32[8,4096]{1,0:T(8,128)}, u32[]{:S(2)}) copy-start(f32[8,4096]{1,0:T(8,128)} %reduce-scatter.5.cloned.1.call-done) | copy-start | bytes 393220
Sparse Core Ops, SparseCore 0:
  18.5 42.2 reduce-scatter.2
  63.3 37.7 reduce-scatter.4
  102.9 158.6 all-gather.4
  263.3 158.9 all-gather.2
where the time goes:
time: 433 us
  waiting for transfers between devices  355 us (82%)
  blocking collectives  30.9 us (7%)
  matrix products  15.5 us (4%)
  between operations  13.9 us (3%)
  other arithmetic  9.81 us (2%)
  local copies, waits for them, and re-layouts  8.03 us (2%)
    all_gather x1, waiting for transfers between devices, local(): lax.all_gather(counts, 'bkt', axis=0, tiled=True)  143 us
    all_gather x1, waiting for transfers between devices, local(): lax.all_gather(deltas, 'bkt', axis=0, tiled=True)  130 us
    reduce_scatter x1, waiting for transfers between devices, local(): lax.psum_scatter(summed[0], 'grp', scatter_dimension=1, tiled=True)  40.8 us
    reduce_scatter x1, waiting for transfers between devices, local(): lax.psum_scatter(summed[1], 'grp', scatter_dimension=1, tiled=True)  40.2 us
    all_gather x1, blocking collectives, local(): lax.all_gather(partner16, 'grp', axis=1, tiled=True)  15.7 us
    all_gather x1, blocking collectives, local(): lax.all_gather(panel_own, 'grp', axis=1, tiled=True)  15.2 us
  transfers between devices with their start and end apart: 4, of which 4 were waited for; matrix products, arithmetic and copies ran while one was open for 4% of the time, Pallas kernels for 0%

commit v1 on v0

v1 whole, which is shorter than its diff:
```python
import jax
import jax.numpy as jnp
from jax import lax
from jax.experimental import pallas as pl
from jax.experimental.pallas import tpu as pltpu
from jax.sharding import PartitionSpec as P

BPO = 8
TILE = 128
RTG = 8
QT = 256
KT = 192
N_BKT = 32
N_GRP = 8
N_ZH = N_GRP // 2
QM = QT // N_GRP
SEG = BPO * QM
META = 16
BLK = KT + META
CHUNK = 16
N_CHUNK = KT // CHUNK
SUM_SCALE = 10240.0
UNIT_SCALE = 65535.0
HALF = 32768
MOVED = BPO * QT

survival_rate = 0.5
f32 = jnp.float32
bf16 = jnp.bfloat16
i32 = jnp.int32
i16 = jnp.int16


def to_code(values, scale):
    return ((values * scale + 0.5).astype(i32) - HALF).astype(i16)


def iota(shape, dim):
    return lax.broadcasted_iota(i32, shape, dim)


def kernel(
    tiles_hbm, row_ref, col_ref, move_ref, pair_ref,
    panel_ref, gains_ref,
    tiles, wide, gath, acc, own, rows, outbox, inbox, rest, pg, look, terms,
    load_sem, s1, f1, r1, q1, s2, r2, s3, f3, r3, q3,
):
    o = lax.axis_index("bkt")
    h = lax.axis_index("grp")
    zh = h // 2
    core = h % 2
    sibling = zh * 2 + (1 - core)

    def load(c):
        part = pl.ds(c * CHUNK, CHUNK)
        return pltpu.make_async_copy(tiles_hbm.at[part], tiles.at[part], load_sem.at[c])

    @pl.loop(0, N_CHUNK)
    def _(c):
        load(c).start()

    barrier = pltpu.get_barrier_semaphore()

    @pl.loop(1, N_BKT)
    def _(d):
        pl.semaphore_signal(barrier, inc=1, device_id=((o + d) % N_BKT, h), device_id_type=pl.DeviceIdType.MESH)

    @pl.loop(1, N_ZH)
    def _(d):
        peer = ((zh + d) % N_ZH) * 2 + core
        pl.semaphore_signal(barrier, inc=1, device_id=(o, peer), device_id_type=pl.DeviceIdType.MESH)

    pl.semaphore_signal(barrier, inc=1, device_id=(o, sibling), device_id_type=pl.DeviceIdType.MESH)

    row = row_ref[...]
    live = row >= 0
    seg_row = jnp.where(live, (row >> 3) * QT + col_ref[...], -1)
    moving = jnp.zeros_like(row)
    for r in range(BPO * RTG):
        moving = jnp.where(row == r, move_ref[r // RTG, r % RTG], moving)
    wide[...] = jnp.full(wide.shape, -1, i32)
    wide[:, :KT] = jnp.where(live, seg_row + MOVED * moving, -1)
    place = iota((META, TILE), 0)
    meta = jnp.where(place == 0, wide[:, :TILE], jnp.where(place == 1, wide[:, TILE:], -1))
    gath[h, KT:BLK, :] = meta.astype(i16)
    diagonal = iota((KT, KT), 0) == iota((KT, KT), 1)
    seg_col = jnp.sum(jnp.where(diagonal, seg_row.astype(f32), 0.0), axis=1, keepdims=True).astype(i32)

    @pl.loop(0, N_CHUNK)
    def _(c):
        load(c).wait()
        sums = jnp.sum(tiles[pl.ds(c * CHUNK, CHUNK)].astype(f32), axis=1)
        gath[h, pl.ds(c * CHUNK, CHUNK), :] = to_code(sums, SUM_SCALE)

    pl.semaphore_wait(barrier, (N_BKT - 1) + (N_ZH - 1) + 1)

    def direct(buf, j, send, recv):
        peer = ((zh + j) % N_ZH) * 2 + core
        return pltpu.make_async_remote_copy(
            src_ref=buf.at[h], dst_ref=buf.at[h], send_sem=send.at[j], recv_sem=recv.at[j],
            device_id=(o, peer), device_id_type=pl.DeviceIdType.MESH,
        )

    def arrived(j):
        return ((zh + N_ZH - j) % N_ZH) * 2 + core

    def arrived_other(j):
        return ((zh + N_ZH - j) % N_ZH) * 2 + (1 - core)

    def pass_on(buf, j, send, recv):
        return pltpu.make_async_remote_copy(
            src_ref=buf.at[arrived(j)], dst_ref=buf.at[arrived(j)], send_sem=send.at[j], recv_sem=recv.at[j],
            device_id=(o, sibling), device_id_type=pl.DeviceIdType.MESH,
        )

    def gather(buf, send, forward, recv, other, use):
        for j in range(1, N_ZH):
            direct(buf, j, send, recv).start()

        @pl.loop(0, N_ZH)
        def _(j):
            @pl.when(j > 0)
            def _():
                pltpu.make_async_remote_copy(
                    src_ref=buf.at[arrived(j)], dst_ref=buf.at[arrived(j)], send_sem=send.at[j], recv_sem=recv.at[j],
                    device_id=(o, sibling), device_id_type=pl.DeviceIdType.MESH,
                ).wait_recv()

            pass_on(buf, j, forward, other).start()
            use(arrived(j))

        @pl.loop(0, N_ZH)
        def _(j):
            pltpu.make_async_remote_copy(
                src_ref=buf.at[arrived_other(j)], dst_ref=buf.at[arrived_other(j)], send_sem=forward.at[j],
                recv_sem=other.at[j], device_id=(o, sibling), device_id_type=pl.DeviceIdType.MESH,
            ).wait_recv()
            use(arrived_other(j))

    def gather_sent(buf, send, forward, recv, other):
        for j in range(1, N_ZH):
            direct(buf, j, send, recv).wait_send()
        for j in range(N_ZH):
            pass_on(buf, j, forward, other).wait_send()

    acc[...] = jnp.zeros_like(acc)
    place = iota((SEG, KT), 0)
    wanted = (place // QM) * QT + h * QM + place % QM

    def count(m):
        code = gath[m, 0:KT, :].astype(i32) + HALF
        high = (code >> 8).astype(f32).astype(bf16)
        low = (code & 255).astype(f32).astype(bf16)
        parts = jnp.concatenate([high, low], axis=1)
        meta = gath[m, KT:BLK, :].astype(i32)
        theirs = jnp.concatenate([meta[0:1], meta[1:2]], axis=1)[:, :KT]
        moved = theirs >= MOVED
        seg = jnp.where(moved, theirs - MOVED, theirs)
        hit = jnp.where(wanted == seg, 1.0, 0.0)
        hit_moved = jnp.where(moved, hit, 0.0)
        mine = jnp.where(seg_col == seg, 1.0, 0.0)
        table = jnp.concatenate([hit, hit_moved, mine], axis=0).astype(bf16)
        acc[...] += jnp.dot(table, parts, preferred_element_type=f32)

    gather(gath, s1, f1, r1, q1, count)

    total = acc[:, :TILE] * (256.0 / SUM_SCALE) + acc[:, TILE:] * (1.0 / SUM_SCALE)
    counts = total[:SEG]
    deltas = total[SEG : 2 * SEG]
    panel_code = to_code(jnp.exp(-survival_rate * counts), UNIT_SCALE).reshape(BPO, QM, TILE)
    delta_code = to_code(jnp.exp(-survival_rate * deltas), UNIT_SCALE).reshape(BPO, QM, TILE)
    rows[:, 0:QM, :] = panel_code
    rows[:, QM : 2 * QM, :] = delta_code

    partner_owner = [pair_ref[o * BPO + p] // BPO for p in range(BPO)]

    def swap(d):
        return pltpu.make_async_remote_copy(
            src_ref=outbox.at[d - 1], dst_ref=inbox.at[d - 1], send_sem=s2.at[d - 1], recv_sem=r2.at[d - 1],
            device_id=((o + d) % N_BKT, h), device_id_type=pl.DeviceIdType.MESH,
        )

    @pl.loop(1, N_BKT)
    def _(d):
        to = (o + d) % N_BKT
        pick = 0
        for p in range(BPO):
            pick = jnp.where(partner_owner[p] == to, p, pick)
        outbox[d - 1] = rows[pick]
        swap(d).start()

    rest[...] = jnp.exp(-survival_rate * (counts - deltas))
    own[...] = jnp.exp(-survival_rate * total[2 * SEG :]).astype(bf16).astype(f32)
    look[...] = jnp.zeros_like(look)

    @pl.loop(1, N_BKT)
    def _(d):
        swap(d).wait_recv()

    for p in range(BPO):
        part = slice(p * QM, (p + 1) * QM)
        got = inbox[jnp.maximum((o - partner_owner[p] + N_BKT) % N_BKT - 1, 0)].astype(i32) + HALF
        got = got.astype(f32) * (1.0 / UNIT_SCALE)
        pg[h, part, :] = got[:QM].astype(bf16)
        panel_ref[part, :] = rest[part, :] * got[QM:]

    place3 = iota((KT, SEG), 1)
    base = (place3 // QM) * QT + place3 % QM

    def fetch(m):
        table = jnp.where(base == seg_col - m * QM, 1.0, 0.0).astype(bf16)
        look[...] += jnp.dot(table, pg[m], preferred_element_type=f32)

    gather(pg, s3, f3, r3, q3, fetch)

    lane = iota((2 * RTG, TILE), 0)

    @pl.loop(0, KT // RTG)
    def _(g):
        k = pl.multiple_of(g * RTG, RTG)
        pair = jnp.concatenate([own[pl.ds(k, RTG), :], look[pl.ds(k, RTG), :]], axis=0).astype(bf16)
        both = jnp.zeros((2 * RTG, TILE), f32)
        for i in range(RTG):
            got = lax.dot_general(
                pair, tiles[k + i], (((1,), (1,)), ((), ())), preferred_element_type=f32
            )
            both = jnp.where(lane % RTG == i, got, both)
        terms[pl.ds(k, RTG), :] = both[:RTG] - both[RTG:]

    spread = jnp.where(iota((BPO * RTG, KT), 0) == row, 1.0, 0.0)
    gains_ref[...] = survival_rate * jnp.dot(
        spread, terms[...], precision=lax.Precision.HIGHEST, preferred_element_type=f32
    )

    gather_sent(gath, s1, f1, r1, q1)
    gather_sent(pg, s3, f3, r3, q3)

    @pl.loop(1, N_BKT)
    def _(d):
        swap(d).wait_send()


def local(record_tiles, tile_row, tile_col, move_blocks, pairing):
    vmem = pl.BlockSpec(memory_space=pltpu.VMEM)
    smem = pl.BlockSpec(memory_space=pltpu.SMEM)
    dma = pltpu.SemaphoreType.DMA
    panel, gains = pl.pallas_call(
        kernel,
        out_shape=(
            jax.ShapeDtypeStruct((SEG, TILE), f32),
            jax.ShapeDtypeStruct((BPO * RTG, TILE), f32),
        ),
        in_specs=[pl.BlockSpec(memory_space=pl.ANY), vmem, vmem, smem, smem],
        out_specs=(vmem, vmem),
        scratch_shapes=[
            pltpu.VMEM((KT, TILE, TILE), bf16),
            pltpu.VMEM((1, 2 * TILE), i32),
            pltpu.VMEM((N_GRP, BLK, TILE), i16),
            pltpu.VMEM((2 * SEG + KT, 2 * TILE), f32),
            pltpu.VMEM((KT, TILE), f32),
            pltpu.VMEM((BPO, 2 * QM, TILE), i16),
            pltpu.VMEM((N_BKT - 1, 2 * QM, TILE), i16),
            pltpu.VMEM((N_BKT - 1, 2 * QM, TILE), i16),
            pltpu.VMEM((SEG, TILE), f32),
            pltpu.VMEM((N_GRP, SEG, TILE), bf16),
            pltpu.VMEM((KT, TILE), f32),
            pltpu.VMEM((KT, TILE), f32),
            dma((N_CHUNK,)),
            dma((N_ZH,)), dma((N_ZH,)), dma((N_ZH,)), dma((N_ZH,)),
            dma((N_BKT - 1,)), dma((N_BKT - 1,)),
            dma((N_ZH,)), dma((N_ZH,)), dma((N_ZH,)), dma((N_ZH,)),
        ],
        compiler_params=pltpu.CompilerParams(
            collective_id=0, has_side_effects=True, vmem_limit_bytes=60 * 1024 * 1024
        ),
        name="swap_round",
    )(record_tiles, tile_row.reshape(1, KT), tile_col.reshape(1, KT), move_blocks, pairing)
    return panel.reshape(BPO, QM * TILE), gains.reshape(BPO, RTG, TILE)


def solution(mesh):
    placed = (
        P(("bkt", "grp"), None, None),
        P(("bkt", "grp")),
        P(("bkt", "grp")),
        P("bkt", "grp"),
        P(),
    )
    return jax.shard_map(
        local,
        mesh=mesh,
        in_specs=placed,
        out_specs=(P("bkt", "grp"), P("bkt", "grp", None)),
        check_vma=False,
    )
```

time: 433 us -> 51.2 us (0.12)
  the two profiles are of different devices: /device:TPU:2 before, /device:TPU:1 now
where the time goes in v1:
time: 51.2 us; the launch traced here: 51 us
  Pallas kernels  47.4 us (93%)
  local copies, waits for them, and re-layouts  2.96 us (6%)
  between operations  0.64 us (1%)
    pallas_call x1, Pallas kernels, local(): pl.pallas_call(kernel, out_shape=(jax.ShapeDtypeStruct((SEG, TILE), f32),...  47.4 us
    reshape x1, local copies, waits for them, and re-layouts, local(): return (panel.reshape(BPO, QM * TILE), gains.reshape(BPO, RTG, TILE))  1.59 us
    unnamed x1, local copies, waits for them, and re-layouts  1.37 us

profile of v1, /device:TPU:1, one launch (start us, length us, event | category | flops | bytes accessed | tf_op | source)
XLA Modules:
  0.0 51.0 jit_solution(15983276888852534567)
XLA Ops:
  0.6 47.4 %swap_round.1 = (f32[256,128]{1,0:T(8,128)}, f32[64,128]{1,0:T(8,128)}) custom-call(bf16[192,128,128]{2,1,0:T(8,128)(2,1)} %tiles_hbm.1, s32[1,192]{1,0:T(1,128)} %bitcast.4, s32[1,192]{1,0:T(1,128)} %bitcast.5, s32[8,8]{1,0:T(8,128)} %move_ref.1, s32[256]{0:T(256)} %pair_ref.1), custom_call_target="tpu_custom_call" | custom-call | tf_op jit(solution)/shard_map/swap_round/pallas_call | solution.py:247
  48.1 1.6 %reshape.18 = f32[8,4096]{1,0:T(8,128)} reshape(f32[256,128]{1,0:T(8,128)} %get-tuple-element.4) | data formatting | bytes 262144 | tf_op jit(solution)/shard_map/reshape | solution.py:278
  49.6 1.4 %copy.8 = f32[8,8,128]{2,1,0:T(8,128)} copy(f32[8,8,128]{2,1,0:T(8,128)} %bitcast.3) | data formatting | bytes 65536

commit v2 on v1

v2 whole, which is shorter than its diff:
```python
import jax
import jax.numpy as jnp
from jax import lax
from jax.experimental import pallas as pl
from jax.experimental.pallas import tpu as pltpu
from jax.sharding import PartitionSpec as P

BPO = 8
TILE = 128
RTG = 8
QT = 256
KT = 192
N_BKT = 32
N_GRP = 8
N_ZH = N_GRP // 2
QM = QT // N_GRP
SEG = BPO * QM
META = 16
BLK = KT + META
CHUNK = 32
N_CHUNK = KT // CHUNK
SUM_SCALE = 10240.0
UNIT_SCALE = 65535.0
HALF = 32768
MOVED = BPO * QT
VMEM_BYTES = 57 * 1024 * 1024

survival_rate = 0.5
f32 = jnp.float32
bf16 = jnp.bfloat16
i32 = jnp.int32
i16 = jnp.int16


def to_code(values, scale):
    return ((values * scale + 0.5).astype(i32) - HALF).astype(i16)


def iota(shape, dim):
    return lax.broadcasted_iota(i32, shape, dim)


def kernel(
    tiles_hbm, row_hbm, col_hbm, move_hbm, pair_hbm,
    panel_ref, gains_ref,
    row_ref, col_ref, move_ref, pair_ref, pick_ref,
    tiles, turned, wide, gath, acc, own, panels, factors, panel_out, far_out, factor_out, panel_in, far_in, factor_in,
    rest, pg, look, terms,
    load_sem, small_sem, s1, f1, r1, q1, s2, r2, s5, r5, s4, r4, s3, f3, r3, q3,
):
    o = lax.axis_index("bkt")
    h = lax.axis_index("grp")
    zh = h // 2
    core = h % 2
    sibling = zh * 2 + (1 - core)

    def far_first(i):
        return (2 + i) * (1 - i // 2) + (3 - i) * (i // 2)

    def owner_at(d):
        y = (o // 8 + far_first(d // 8)) % 4
        z = (o // 4 + 1 - d % 2) % 2
        x = (o + far_first((d // 2) % 4)) % 4
        return y * 8 + z * 4 + x

    def load(c):
        part = pl.ds(c * CHUNK, CHUNK)
        return pltpu.make_async_copy(tiles_hbm.at[part], tiles.at[part], load_sem.at[c])

    small = [
        pltpu.make_async_copy(src, dst, small_sem.at[i])
        for i, (src, dst) in enumerate(
            ((row_hbm, row_ref), (col_hbm, col_ref), (move_hbm, move_ref), (pair_hbm, pair_ref))
        )
    ]
    for copy in small:
        copy.start()

    @pl.loop(0, N_CHUNK)
    def _(c):
        load(c).start()

    barrier = pltpu.get_barrier_semaphore()

    for j in (2, 1, 3):
        peer = ((zh + j) % N_ZH) * 2 + core
        pl.semaphore_signal(barrier, inc=1, device_id=(o, peer), device_id_type=pl.DeviceIdType.MESH)

    @pl.loop(0, N_BKT - 1)
    def _(d):
        pl.semaphore_signal(barrier, inc=1, device_id=(owner_at(d), h), device_id_type=pl.DeviceIdType.MESH)

    pl.semaphore_signal(barrier, inc=1, device_id=(o, sibling), device_id_type=pl.DeviceIdType.MESH)

    for copy in small:
        copy.wait()

    row = row_ref[...]
    live = row >= 0
    seg_row = jnp.where(live, (row >> 3) * QT + col_ref[...], -1)
    moving = jnp.zeros_like(row)
    for r in range(BPO * RTG):
        moving = jnp.where(row == r, move_ref[r // RTG, r % RTG], moving)
    wide[...] = jnp.full(wide.shape, -1, i32)
    wide[:, :KT] = jnp.where(live, seg_row + MOVED * moving, -1)
    place = iota((META, TILE), 0)
    meta = jnp.where(place == 0, wide[:, :TILE], jnp.where(place == 1, wide[:, TILE:], -1))
    gath[h, 0:META, :] = meta.astype(i16)

    panel_in[o] = jnp.zeros(panel_in.shape[1:], bf16)
    far_in[o] = jnp.zeros(far_in.shape[1:], bf16)
    factor_in[o] = jnp.zeros(factor_in.shape[1:], i16)

    def column_sums(c):
        load(c).wait()

        @pl.loop(0, CHUNK // META)
        def _(e):
            k = pl.multiple_of(c * CHUNK + e * META, META)
            sums = jnp.sum(tiles[pl.ds(k, META)].astype(f32), axis=1)
            gath[h, pl.ds(META + k, META), :] = to_code(sums, SUM_SCALE)

    order = (2, 1, 3)

    def arrived(j):
        return ((zh + N_ZH - j) % N_ZH) * 2 + core

    def arrived_other(j):
        return ((zh + N_ZH - j) % N_ZH) * 2 + (1 - core)

    def hop(buf, part, block, to, send_sem, recv_sem):
        ref = buf.at[block, part]
        return pltpu.make_async_remote_copy(
            src_ref=ref, dst_ref=ref, send_sem=send_sem, recv_sem=recv_sem,
            device_id=(o, to), device_id_type=pl.DeviceIdType.MESH,
        )

    def send_own(buf, part, x, send, forward, recv, other):
        for j in order:
            hop(buf, part, h, ((zh + j) % N_ZH) * 2 + core, send.at[x, j], recv.at[x, j]).start()
        hop(buf, part, h, sibling, forward.at[x, 0], other.at[x, 0]).start()

    def pass_on(buf, part, x, j, send, forward, recv, other):
        hop(buf, part, arrived(j), sibling, send.at[x, j], recv.at[x, j]).wait_recv()
        hop(buf, part, arrived(j), sibling, forward.at[x, j], other.at[x, j]).start()

    def from_other(buf, part, x, j, forward, other):
        hop(buf, part, arrived_other(j), sibling, forward.at[x, j], other.at[x, j]).wait_recv()

    def all_sent(buf, part, x, send, forward, recv, other):
        for j in order:
            hop(buf, part, h, ((zh + j) % N_ZH) * 2 + core, send.at[x, j], recv.at[x, j]).wait_send()
        for j in range(N_ZH):
            hop(buf, part, arrived(j), sibling, forward.at[x, j], other.at[x, j]).wait_send()

    def in_order(i):
        return i + (i // 2) * (5 - 2 * i)

    first = (gath, pl.ds(0, BLK), 0, s1, f1, r1, q1)

    for c in range(N_CHUNK):
        column_sums(c)
    pl.semaphore_wait(barrier, (N_BKT - 1) + (N_ZH - 1) + 1)
    send_own(*first)

    diagonal = iota((KT, KT), 0) == iota((KT, KT), 1)
    seg_col = jnp.sum(jnp.where(diagonal, seg_row.astype(f32), 0.0), axis=1, keepdims=True).astype(i32)
    acc[...] = jnp.zeros_like(acc)
    place = iota((SEG, KT), 0)
    far = arrived(2)
    wanted = (place // QM) * QT + h * QM + place % QM
    wanted_far = wanted + (far - h) * QM

    partner_owner = [pair_ref[o * BPO + p] // BPO for p in range(BPO)]

    @pl.loop(0, N_BKT - 1)
    def _(d):
        to = owner_at(d)
        pick = 0
        for p in range(BPO):
            pick = jnp.where(partner_owner[p] == to, p, pick)
        pick_ref[d] = pick

    def count(m):
        code = gath[m, META:BLK, :].astype(i32) + HALF
        high = (code >> 8).astype(f32).astype(bf16)
        low = (code & 255).astype(f32).astype(bf16)
        parts = jnp.concatenate([high, low], axis=1)
        meta = gath[m, 0:META, :].astype(i32)
        theirs = jnp.concatenate([meta[0:1], meta[1:2]], axis=1)[:, :KT]
        moved = theirs >= MOVED
        seg = jnp.where(moved, theirs - MOVED, theirs)
        hit = jnp.where(wanted == seg, 1.0, 0.0)
        hit_moved = jnp.where(moved, hit, 0.0)
        hit_far = jnp.where(wanted_far == seg, 1.0, 0.0)
        mine = jnp.where(seg_col == seg, 1.0, 0.0)
        table = jnp.concatenate([hit, hit_far, hit_moved, mine], axis=0).astype(bf16)
        acc[...] += jnp.dot(table, parts, preferred_element_type=f32)

    @pl.loop(0, KT // 4)
    def _(g):
        for b in range(2):
            for a in range(2):
                turned[g, a * TILE : (a + 1) * TILE, b * TILE : (b + 1) * TILE] = tiles[4 * g + 2 * b + a].T

    @pl.loop(0, N_ZH)
    def _(i):
        count(arrived(in_order(i)))

        @pl.when(i < N_ZH - 1)
        def _():
            j = in_order(i + 1)
            pass_on(*first[:3], j, *first[3:])

        j = in_order(i)
        from_other(*first[:3], j, f1, q1)
        count(arrived_other(j))

    total = acc[:, :TILE] * (256.0 / SUM_SCALE) + acc[:, TILE:] * (1.0 / SUM_SCALE)
    counts = total[:SEG]
    deltas = total[2 * SEG : 3 * SEG]
    both = jnp.exp(-survival_rate * total[: 2 * SEG]).astype(bf16)
    panels[:, 0:QM, :] = both[:SEG].reshape(BPO, QM, TILE)
    panels[:, QM : 2 * QM, :] = both[SEG:].reshape(BPO, QM, TILE)

    def swap(outbox, inbox, d, send, recv):
        return pltpu.make_async_remote_copy(
            src_ref=outbox.at[d], dst_ref=inbox.at[o], send_sem=send.at[d], recv_sem=recv.at[d],
            device_id=(owner_at(d), h), device_id_type=pl.DeviceIdType.MESH,
        )

    def swapped(inbox, d, send, recv):
        y = (o // 8 + 4 - far_first(d // 8)) % 4
        z = (o // 4 + 1 - d % 2) % 2
        x = (o + 4 - far_first((d // 2) % 4)) % 4
        slot = inbox.at[y * 8 + z * 4 + x]
        return pltpu.make_async_remote_copy(
            src_ref=slot, dst_ref=slot, send_sem=send.at[d], recv_sem=recv.at[d],
            device_id=(owner_at(d), h), device_id_type=pl.DeviceIdType.MESH,
        )

    @pl.loop(0, N_BKT - 1)
    def _(d):
        panel_out[d] = panels[pick_ref[d], 0:QM]
        swap(panel_out, panel_in, d, s2, r2).start()

    @pl.loop(0, N_BKT - 1)
    def _(d):
        far_out[d] = panels[pick_ref[d], QM : 2 * QM]
        swap(far_out, far_in, d, s5, r5).start()

    factors[...] = to_code(jnp.exp(-survival_rate * deltas), UNIT_SCALE).reshape(BPO, QM, TILE)

    rest[...] = jnp.exp(-survival_rate * (counts - deltas))
    own[...] = jnp.exp(-survival_rate * total[3 * SEG :]).astype(bf16).astype(f32)
    look[...] = jnp.zeros_like(look)

    @pl.loop(0, N_BKT - 1)
    def _(d):
        swapped(panel_in, d, s2, r2).wait_recv()

    for p in range(BPO):
        part = slice(p * QM, (p + 1) * QM)
        pg[h, part, :] = panel_in[partner_owner[p]]

    near = (1, 3)
    for j in near:
        hop(pg, pl.ds(0, SEG), h, ((zh + j) % N_ZH) * 2 + core, s3.at[j], r3.at[j]).start()

    def to_other(j):
        return hop(pg, pl.ds(0, SEG), arrived(j), sibling, f3.at[j], q3.at[j])

    def at_other(j):
        return hop(pg, pl.ds(0, SEG), arrived_other(j), sibling, f3.at[j], q3.at[j])

    to_other(0).start()

    @pl.loop(0, N_BKT - 1)
    def _(d):
        swapped(far_in, d, s5, r5).wait_recv()

    for p in range(BPO):
        pg[far, p * QM : (p + 1) * QM, :] = far_in[partner_owner[p]]

    to_other(2).start()

    @pl.loop(0, N_BKT - 1)
    def _(d):
        factor_out[d] = factors[pick_ref[d]]
        swap(factor_out, factor_in, d, s4, r4).start()

    place3 = iota((KT, SEG), 1)
    base = (place3 // QM) * QT + place3 % QM

    def fetch(m):
        table = jnp.where(base == seg_col - m * QM, 1.0, 0.0).astype(bf16)
        look[...] += jnp.dot(table, pg[m], preferred_element_type=f32)

    @pl.loop(0, 2)
    def _(i):
        fetch(arrived(2 * i))
        at_other(2 * i).wait_recv()
        fetch(arrived_other(2 * i))

    for j in near:
        hop(pg, pl.ds(0, SEG), arrived(j), sibling, s3.at[j], r3.at[j]).wait_recv()
        to_other(j).start()

    @pl.loop(0, 2)
    def _(i):
        fetch(arrived(2 * i + 1))

    @pl.loop(0, 2)
    def _(i):
        at_other(2 * i + 1).wait_recv()
        fetch(arrived_other(2 * i + 1))

    lane = iota((2 * RTG, TILE), 0) % RTG
    even = lane % 2 == 0
    across = (lane // 2) % 2
    down = lane // 4

    @pl.loop(0, KT // (4 * RTG))
    def _(g):
        for x in range(4):
            k = pl.multiple_of(g * 4 * RTG + x * RTG, RTG)
            pair = jnp.concatenate([own[pl.ds(k, RTG), :], look[pl.ds(k, RTG), :]], axis=0)
            split = jnp.concatenate([jnp.where(even, pair, 0.0), jnp.where(even, 0.0, pair)], axis=1).astype(bf16)
            both = jnp.zeros((2 * RTG, TILE), f32)
            for y in range(2):
                got = jnp.dot(split, turned[g * RTG + x * 2 + y], preferred_element_type=f32)
                got = jnp.where(across == 0, got[:, :TILE], got[:, TILE:])
                both = jnp.where(down == y, got, both)
            terms[pl.ds(k, RTG), :] = both[:RTG] - both[RTG:]

    spread = jnp.where(iota((BPO * RTG, KT), 0) == row, 1.0, 0.0).astype(bf16)
    term = terms[...]
    high = term.astype(bf16)
    term = term - high.astype(f32)
    mid = term.astype(bf16)
    low = (term - mid.astype(f32)).astype(bf16)
    summed = jnp.dot(spread, jnp.concatenate([high, mid, low], axis=1), preferred_element_type=f32)
    gains_ref[...] = survival_rate * (summed[:, :TILE] + summed[:, TILE : 2 * TILE] + summed[:, 2 * TILE :])

    @pl.loop(0, N_BKT - 1)
    def _(d):
        swapped(factor_in, d, s4, r4).wait_recv()

    for p in range(BPO):
        part = slice(p * QM, (p + 1) * QM)
        got = (factor_in[partner_owner[p]].astype(i32) + HALF).astype(f32) * (1.0 / UNIT_SCALE)
        rest[part, :] = rest[part, :] * got

    for t in range(QM):
        panel_ref[:, t * TILE : (t + 1) * TILE] = rest[pl.ds(t, BPO, stride=QM), :]

    all_sent(*first)
    for j in near:
        hop(pg, pl.ds(0, SEG), h, ((zh + j) % N_ZH) * 2 + core, s3.at[j], r3.at[j]).wait_send()
    for j in range(N_ZH):
        to_other(j).wait_send()

    @pl.loop(0, N_BKT - 1)
    def _(d):
        swap(panel_out, panel_in, d, s2, r2).wait_send()
        swap(far_out, far_in, d, s5, r5).wait_send()
        swap(factor_out, factor_in, d, s4, r4).wait_send()


def hand_over(panel_ref, gains_ref, panel_out, gains_out):
    panel_out[...] = panel_ref[...]
    gains_out[...] = gains_ref[...]


def local(record_tiles, tile_row, tile_col, move_blocks, pairing):
    vmem = pl.BlockSpec(memory_space=pltpu.VMEM)
    hbm = pl.BlockSpec(memory_space=pltpu.HBM)
    dma = pltpu.SemaphoreType.DMA
    panel, gains = pl.pallas_call(
        kernel,
        out_shape=(
            jax.ShapeDtypeStruct((BPO, QM * TILE), f32),
            jax.ShapeDtypeStruct((BPO * RTG, TILE), f32),
        ),
        in_specs=[hbm] * 5,
        out_specs=(vmem, vmem),
        scratch_shapes=[
            pltpu.VMEM((1, KT), i32),
            pltpu.VMEM((1, KT), i32),
            pltpu.SMEM((BPO, RTG), i32),
            pltpu.SMEM((N_BKT * BPO,), i32),
            pltpu.SMEM((N_BKT,), i32),
            pltpu.VMEM((KT, TILE, TILE), bf16),
            pltpu.VMEM((KT // 4, 2 * TILE, 2 * TILE), bf16),
            pltpu.VMEM((1, 2 * TILE), i32),
            pltpu.VMEM((N_GRP, BLK, TILE), i16),
            pltpu.VMEM((3 * SEG + KT, 2 * TILE), f32),
            pltpu.VMEM((KT, TILE), f32),
            pltpu.VMEM((BPO, 2 * QM, TILE), bf16),
            pltpu.VMEM((BPO, QM, TILE), i16),
            pltpu.VMEM((N_BKT - 1, QM, TILE), bf16),
            pltpu.VMEM((N_BKT - 1, QM, TILE), bf16),
            pltpu.VMEM((N_BKT - 1, QM, TILE), i16),
            pltpu.VMEM((N_BKT, QM, TILE), bf16),
            pltpu.VMEM((N_BKT, QM, TILE), bf16),
            pltpu.VMEM((N_BKT, QM, TILE), i16),
            pltpu.VMEM((SEG, TILE), f32),
            pltpu.VMEM((N_GRP, SEG, TILE), bf16),
            pltpu.VMEM((KT, TILE), f32),
            pltpu.VMEM((KT, TILE), f32),
            dma((N_CHUNK,)),
            dma((4,)),
            dma((1, N_ZH)), dma((1, N_ZH)), dma((1, N_ZH)), dma((1, N_ZH)),
            dma((N_BKT - 1,)), dma((N_BKT - 1,)), dma((N_BKT - 1,)),
            dma((N_BKT - 1,)), dma((N_BKT - 1,)), dma((N_BKT - 1,)),
            dma((N_ZH,)), dma((N_ZH,)), dma((N_ZH,)), dma((N_ZH,)),
        ],
        compiler_params=pltpu.CompilerParams(
            collective_id=0, has_side_effects=True, vmem_limit_bytes=VMEM_BYTES
        ),
        name="swap_round",
    )(record_tiles, tile_row.reshape(1, KT), tile_col.reshape(1, KT), move_blocks, pairing)
    return pl.pallas_call(
        hand_over,
        out_shape=(
            jax.ShapeDtypeStruct((BPO, QM * TILE), f32),
            jax.ShapeDtypeStruct((BPO, RTG, TILE), f32),
        ),
        in_specs=[vmem, vmem],
        out_specs=(vmem, vmem),
        compiler_params=pltpu.CompilerParams(vmem_limit_bytes=VMEM_BYTES),
        name="hand_over",
    )(panel, gains.reshape(BPO, RTG, TILE))


def solution(mesh):
    placed = (
        P(("bkt", "grp"), None, None),
        P(("bkt", "grp")),
        P(("bkt", "grp")),
        P("bkt", "grp"),
        P(),
    )
    return jax.shard_map(
        local,
        mesh=mesh,
        in_specs=placed,
        out_specs=(P("bkt", "grp"), P("bkt", "grp", None)),
        check_vma=False,
    )
```

time: 51.2 us -> 42.6 us (0.83)
  Pallas kernels: 47.4 us -> 41.6 us
  local copies, waits for them, and re-layouts: 2.96 us -> 0 us
    pallas_call x1 -> x2, Pallas kernels: 47.4 us -> 41.6 us  [the longest x1 40 us: local(): pl.pallas_call(kernel, out_shape=(jax.ShapeDtypeStruct((BPO, QM * TILE),...]
    reshape x1 -> x0, local copies, waits for them, and re-layouts: 1.59 us -> none  [local(): return (panel.reshape(BPO, QM * TILE), gains.reshape(BPO, RTG, TILE))]
    unnamed x1 -> x0, local copies, waits for them, and re-layouts: 1.37 us -> none
where the time goes in v2:
time: 42.6 us; the launch traced here: 42.2 us
  Pallas kernels  41.6 us (98%)
  between operations  0.64 us (2%)
    pallas_call x1, Pallas kernels, local(): pl.pallas_call(kernel, out_shape=(jax.ShapeDtypeStruct((BPO, QM * TILE),...  40 us
    pallas_call x1, Pallas kernels, local(): pl.pallas_call(hand_over, out_shape=(jax.ShapeDtypeStruct((BPO, QM * TILE...  1.57 us

profile of v2, /device:TPU:1, one launch (start us, length us, event | category | flops | bytes accessed | tf_op | source)
XLA Modules:
  0.0 42.2 jit_solution(8037474778356375504)
XLA Ops:
  0.6 40.0 %swap_round.1 = (f32[8,4096]{1,0:T(8,128)}, f32[64,128]{1,0:T(8,128)}) custom-call(bf16[192,128,128]{2,1,0:T(8,128)(2,1)} %tiles_hbm.1, s32[1,192]{1,0:T(1,128)} %bitcast.4, s32[1,192]{1,0:T(1,128)} %bitcast.5, s32[8,8]{1,0:T(8,128)} %move_hbm.1, s32[256]{0:T(256)} %pair_hbm.1), custom_call_target="tpu_custom_call" | custom-call | tf_op jit(solution)/shard_map/swap_round/pallas_call | solution.py:379
  40.6 1.6 %hand_over.1 = (f32[8,4096]{1,0:T(8,128)}, f32[8,8,128]{2,1,0:T(8,128)}) custom-call(f32[8,4096]{1,0:T(8,128)} %get-tuple-element.4.panel_ref, f32[8,8,128]{2,1,0:T(8,128)} %bitcast.3), custom_call_target="tpu_custom_call" | custom-call | tf_op jit(solution)/shard_map/hand_over/pallas_call | solution.py:423

commit v3 on v2

--- a/solution.py
+++ b/solution.py
@@ -43,7 +43,7 @@
 def kernel(
     tiles_hbm, row_hbm, col_hbm, move_hbm, pair_hbm,
     panel_ref, gains_ref,
-    row_ref, col_ref, move_ref, pair_ref, pick_ref,
+    row_ref, col_ref, move_ref, pair_ref, pick_ref, slot_ref,
     tiles, turned, wide, gath, acc, own, panels, factors, panel_out, far_out, factor_out, panel_in, far_in, factor_in,
     rest, pg, look, terms,
     load_sem, small_sem, s1, f1, r1, q1, s2, r2, s5, r5, s4, r4, s3, f3, r3, q3,
@@ -107,10 +107,6 @@
     meta = jnp.where(place == 0, wide[:, :TILE], jnp.where(place == 1, wide[:, TILE:], -1))
     gath[h, 0:META, :] = meta.astype(i16)
 
-    panel_in[o] = jnp.zeros(panel_in.shape[1:], bf16)
-    far_in[o] = jnp.zeros(far_in.shape[1:], bf16)
-    factor_in[o] = jnp.zeros(factor_in.shape[1:], i16)
-
     def column_sums(c):
         load(c).wait()
 
@@ -173,6 +169,8 @@
 
     partner_owner = [pair_ref[o * BPO + p] // BPO for p in range(BPO)]
 
+    slot_ref[o] = 0
+
     @pl.loop(0, N_BKT - 1)
     def _(d):
         to = owner_at(d)
@@ -180,6 +178,10 @@
         for p in range(BPO):
             pick = jnp.where(partner_owner[p] == to, p, pick)
         pick_ref[d] = pick
+        y = (o // 8 + 4 - far_first(d // 8)) % 4
+        z = (o // 4 + 1 - d % 2) % 2
+        x = (o + 4 - far_first((d // 2) % 4)) % 4
+        slot_ref[y * 8 + z * 4 + x] = d
 
     def count(m):
         code = gath[m, META:BLK, :].astype(i32) + HALF
@@ -225,22 +227,17 @@
 
     def swap(outbox, inbox, d, send, recv):
         return pltpu.make_async_remote_copy(
-            src_ref=outbox.at[d], dst_ref=inbox.at[o], send_sem=send.at[d], recv_sem=recv.at[d],
+            src_ref=outbox.at[d], dst_ref=inbox.at[d], send_sem=send.at[0], recv_sem=recv.at[0],
             device_id=(owner_at(d), h), device_id_type=pl.DeviceIdType.MESH,
         )
 
-    def swapped(inbox, d, send, recv):
-        y = (o // 8 + 4 - far_first(d // 8)) % 4
-        z = (o // 4 + 1 - d % 2) % 2
-        x = (o + 4 - far_first((d // 2) % 4)) % 4
-        slot = inbox.at[y * 8 + z * 4 + x]
+    def all_swaps(outbox, inbox, send, recv):
         return pltpu.make_async_remote_copy(
-            src_ref=slot, dst_ref=slot, send_sem=send.at[d], recv_sem=recv.at[d],
-            device_id=(owner_at(d), h), device_id_type=pl.DeviceIdType.MESH,
+            src_ref=outbox, dst_ref=inbox, send_sem=send.at[0], recv_sem=recv.at[0],
+            device_id=(owner_at(0), h), device_id_type=pl.DeviceIdType.MESH,
         )
 
-    @pl.loop(0, N_BKT - 1)
-    def _(d):
+    for d in range(N_BKT - 1):
         panel_out[d] = panels[pick_ref[d], 0:QM]
         swap(panel_out, panel_in, d, s2, r2).start()
 
@@ -255,13 +252,12 @@
     own[...] = jnp.exp(-survival_rate * total[3 * SEG :]).astype(bf16).astype(f32)
     look[...] = jnp.zeros_like(look)
 
-    @pl.loop(0, N_BKT - 1)
-    def _(d):
-        swapped(panel_in, d, s2, r2).wait_recv()
+    source = [slot_ref[partner_owner[p]] for p in range(BPO)]
+    all_swaps(panel_out, panel_in, s2, r2).wait_recv()
 
     for p in range(BPO):
         part = slice(p * QM, (p + 1) * QM)
-        pg[h, part, :] = panel_in[partner_owner[p]]
+        pg[h, part, :] = panel_in[source[p]]
 
     near = (1, 3)
     for j in near:
@@ -275,12 +271,10 @@
 
     to_other(0).start()
 
-    @pl.loop(0, N_BKT - 1)
-    def _(d):
-        swapped(far_in, d, s5, r5).wait_recv()
+    all_swaps(far_out, far_in, s5, r5).wait_recv()
 
     for p in range(BPO):
-        pg[far, p * QM : (p + 1) * QM, :] = far_in[partner_owner[p]]
+        pg[far, p * QM : (p + 1) * QM, :] = far_in[source[p]]
 
     to_other(2).start()
 
@@ -302,6 +296,9 @@
         at_other(2 * i).wait_recv()
         fetch(arrived_other(2 * i))
 
+    all_sent(*first)
+    all_swaps(panel_out, panel_in, s2, r2).wait_send()
+    all_swaps(far_out, far_in, s5, r5).wait_send()
     for j in near:
         hop(pg, pl.ds(0, SEG), arrived(j), sibling, s3.at[j], r3.at[j]).wait_recv()
         to_other(j).start()
@@ -342,29 +339,22 @@
     summed = jnp.dot(spread, jnp.concatenate([high, mid, low], axis=1), preferred_element_type=f32)
     gains_ref[...] = survival_rate * (summed[:, :TILE] + summed[:, TILE : 2 * TILE] + summed[:, 2 * TILE :])
 
-    @pl.loop(0, N_BKT - 1)
-    def _(d):
-        swapped(factor_in, d, s4, r4).wait_recv()
+    all_swaps(factor_out, factor_in, s4, r4).wait_recv()
 
     for p in range(BPO):
         part = slice(p * QM, (p + 1) * QM)
-        got = (factor_in[partner_owner[p]].astype(i32) + HALF).astype(f32) * (1.0 / UNIT_SCALE)
+        got = (factor_in[source[p]].astype(i32) + HALF).astype(f32) * (1.0 / UNIT_SCALE)
         rest[part, :] = rest[part, :] * got
 
     for t in range(QM):
         panel_ref[:, t * TILE : (t + 1) * TILE] = rest[pl.ds(t, BPO, stride=QM), :]
 
-    all_sent(*first)
     for j in near:
         hop(pg, pl.ds(0, SEG), h, ((zh + j) % N_ZH) * 2 + core, s3.at[j], r3.at[j]).wait_send()
     for j in range(N_ZH):
         to_other(j).wait_send()
 
-    @pl.loop(0, N_BKT - 1)
-    def _(d):
-        swap(panel_out, panel_in, d, s2, r2).wait_send()
-        swap(far_out, far_in, d, s5, r5).wait_send()
-        swap(factor_out, factor_in, d, s4, r4).wait_send()
+    all_swaps(factor_out, factor_in, s4, r4).wait_send()
 
 
 def hand_over(panel_ref, gains_ref, panel_out, gains_out):
@@ -390,6 +380,7 @@
             pltpu.SMEM((BPO, RTG), i32),
             pltpu.SMEM((N_BKT * BPO,), i32),
             pltpu.SMEM((N_BKT,), i32),
+            pltpu.SMEM((N_BKT,), i32),
             pltpu.VMEM((KT, TILE, TILE), bf16),
             pltpu.VMEM((KT // 4, 2 * TILE, 2 * TILE), bf16),
             pltpu.VMEM((1, 2 * TILE), i32),
@@ -401,9 +392,9 @@
             pltpu.VMEM((N_BKT - 1, QM, TILE), bf16),
             pltpu.VMEM((N_BKT - 1, QM, TILE), bf16),
             pltpu.VMEM((N_BKT - 1, QM, TILE), i16),
-            pltpu.VMEM((N_BKT, QM, TILE), bf16),
-            pltpu.VMEM((N_BKT, QM, TILE), bf16),
-            pltpu.VMEM((N_BKT, QM, TILE), i16),
+            pltpu.VMEM((N_BKT - 1, QM, TILE), bf16),
+            pltpu.VMEM((N_BKT - 1, QM, TILE), bf16),
+            pltpu.VMEM((N_BKT - 1, QM, TILE), i16),
             pltpu.VMEM((SEG, TILE), f32),
             pltpu.VMEM((N_GRP, SEG, TILE), bf16),
             pltpu.VMEM((KT, TILE), f32),
@@ -411,8 +402,7 @@
             dma((N_CHUNK,)),
             dma((4,)),
             dma((1, N_ZH)), dma((1, N_ZH)), dma((1, N_ZH)), dma((1, N_ZH)),
-            dma((N_BKT - 1,)), dma((N_BKT - 1,)), dma((N_BKT - 1,)),
-            dma((N_BKT - 1,)), dma((N_BKT - 1,)), dma((N_BKT - 1,)),
+            dma((1,)), dma((1,)), dma((1,)), dma((1,)), dma((1,)), dma((1,)),
             dma((N_ZH,)), dma((N_ZH,)), dma((N_ZH,)), dma((N_ZH,)),
         ],
         compiler_params=pltpu.CompilerParams(

time: 42.6 us -> 40.6 us (0.953)
  Pallas kernels: 41.6 us -> 39.8 us
    pallas_call x1, Pallas kernels: 40 us -> 38.3 us  [local(): pl.pallas_call(kernel, out_shape=(jax.ShapeDtypeStruct((BPO, QM * TILE),...]
where the time goes in v3:
time: 40.6 us; the launch traced here: 40.5 us
  Pallas kernels  39.8 us (98%)
  between operations  0.64 us (2%)
    pallas_call x1, Pallas kernels, local(): pl.pallas_call(kernel, out_shape=(jax.ShapeDtypeStruct((BPO, QM * TILE),...  38.3 us
    pallas_call x1, Pallas kernels, local(): pl.pallas_call(hand_over, out_shape=(jax.ShapeDtypeStruct((BPO, QM * TILE...  1.57 us

profile of v3, /device:TPU:1, one launch (start us, length us, event | category | flops | bytes accessed | tf_op | source)
XLA Modules:
  0.0 40.5 jit_solution(5301379870759697561)
XLA Ops:
  0.6 38.3 %swap_round.1 = (f32[8,4096]{1,0:T(8,128)}, f32[64,128]{1,0:T(8,128)}) custom-call(bf16[192,128,128]{2,1,0:T(8,128)(2,1)} %tiles_hbm.1, s32[1,192]{1,0:T(1,128)} %bitcast.4, s32[1,192]{1,0:T(1,128)} %bitcast.5, s32[8,8]{1,0:T(8,128)} %move_hbm.1, s32[256]{0:T(256)} %pair_hbm.1), custom_call_target="tpu_custom_call" | custom-call | tf_op jit(solution)/shard_map/swap_round/pallas_call | solution.py:369
  38.9 1.6 %hand_over.1 = (f32[8,4096]{1,0:T(8,128)}, f32[8,8,128]{2,1,0:T(8,128)}) custom-call(f32[8,4096]{1,0:T(8,128)} %get-tuple-element.4.panel_ref, f32[8,8,128]{2,1,0:T(8,128)} %bitcast.3), custom_call_target="tpu_custom_call" | custom-call | tf_op jit(solution)/shard_map/hand_over/pallas_call | solution.py:413

commit v4 on v3

--- a/solution.py
+++ b/solution.py
@@ -67,6 +67,9 @@
         part = pl.ds(c * CHUNK, CHUNK)
         return pltpu.make_async_copy(tiles_hbm.at[part], tiles.at[part], load_sem.at[c])
 
+    for c in range(N_CHUNK):
+        load(c).start()
+
     small = [
         pltpu.make_async_copy(src, dst, small_sem.at[i])
         for i, (src, dst) in enumerate(
@@ -76,18 +79,13 @@
     for copy in small:
         copy.start()
 
-    @pl.loop(0, N_CHUNK)
-    def _(c):
-        load(c).start()
-
     barrier = pltpu.get_barrier_semaphore()
 
     for j in (2, 1, 3):
         peer = ((zh + j) % N_ZH) * 2 + core
         pl.semaphore_signal(barrier, inc=1, device_id=(o, peer), device_id_type=pl.DeviceIdType.MESH)
 
-    @pl.loop(0, N_BKT - 1)
-    def _(d):
+    for d in range(N_BKT - 1):
         pl.semaphore_signal(barrier, inc=1, device_id=(owner_at(d), h), device_id_type=pl.DeviceIdType.MESH)
 
     pl.semaphore_signal(barrier, inc=1, device_id=(o, sibling), device_id_type=pl.DeviceIdType.MESH)
@@ -110,11 +108,9 @@
     def column_sums(c):
         load(c).wait()
 
-        @pl.loop(0, CHUNK // META)
-        def _(e):
-            k = pl.multiple_of(c * CHUNK + e * META, META)
-            sums = jnp.sum(tiles[pl.ds(k, META)].astype(f32), axis=1)
-            gath[h, pl.ds(META + k, META), :] = to_code(sums, SUM_SCALE)
+        for k in range(c * CHUNK, (c + 1) * CHUNK, META):
+            sums = jnp.sum(tiles[k : k + META].astype(f32), axis=1)
+            gath[h, META + k : 2 * META + k, :] = to_code(sums, SUM_SCALE)
 
     order = (2, 1, 3)
 
@@ -221,9 +217,7 @@
     total = acc[:, :TILE] * (256.0 / SUM_SCALE) + acc[:, TILE:] * (1.0 / SUM_SCALE)
     counts = total[:SEG]
     deltas = total[2 * SEG : 3 * SEG]
-    both = jnp.exp(-survival_rate * total[: 2 * SEG]).astype(bf16)
-    panels[:, 0:QM, :] = both[:SEG].reshape(BPO, QM, TILE)
-    panels[:, QM : 2 * QM, :] = both[SEG:].reshape(BPO, QM, TILE)
+    panels[:, 0:QM, :] = jnp.exp(-survival_rate * counts).astype(bf16).reshape(BPO, QM, TILE)
 
     def swap(outbox, inbox, d, send, recv):
         return pltpu.make_async_remote_copy(
@@ -241,8 +235,10 @@
         panel_out[d] = panels[pick_ref[d], 0:QM]
         swap(panel_out, panel_in, d, s2, r2).start()
 
-    @pl.loop(0, N_BKT - 1)
-    def _(d):
+    far_panels = jnp.exp(-survival_rate * total[SEG : 2 * SEG]).astype(bf16)
+    panels[:, QM : 2 * QM, :] = far_panels.reshape(BPO, QM, TILE)
+
+    for d in range(N_BKT - 1):
         far_out[d] = panels[pick_ref[d], QM : 2 * QM]
         swap(far_out, far_in, d, s5, r5).start()
 
@@ -278,8 +274,7 @@
 
     to_other(2).start()
 
-    @pl.loop(0, N_BKT - 1)
-    def _(d):
+    for d in range(N_BKT - 1):
         factor_out[d] = factors[pick_ref[d]]
         swap(factor_out, factor_in, d, s4, r4).start()
 

time: 40.6 us -> 40.5 us (level)
  no operation moved by 1% of the time
where the time goes in v4:
time: 40.5 us; the launch traced here: 40.4 us
  Pallas kernels  39.8 us (98%)
  between operations  0.64 us (2%)
    pallas_call x1, Pallas kernels, local(): pl.pallas_call(kernel, out_shape=(jax.ShapeDtypeStruct((BPO, QM * TILE),...  38.2 us
    pallas_call x1, Pallas kernels, local(): pl.pallas_call(hand_over, out_shape=(jax.ShapeDtypeStruct((BPO, QM * TILE...  1.57 us

profile of v4, /device:TPU:1, one launch (start us, length us, event | category | flops | bytes accessed | tf_op | source)
XLA Modules:
  0.0 40.4 jit_solution(510590430638698870)
XLA Ops:
  0.6 38.2 %swap_round.1 = (f32[8,4096]{1,0:T(8,128)}, f32[64,128]{1,0:T(8,128)}) custom-call(bf16[192,128,128]{2,1,0:T(8,128)(2,1)} %tiles_hbm.1, s32[1,192]{1,0:T(1,128)} %bitcast.4, s32[1,192]{1,0:T(1,128)} %bitcast.5, s32[8,8]{1,0:T(8,128)} %move_hbm.1, s32[256]{0:T(256)} %pair_hbm.1), custom_call_target="tpu_custom_call" | custom-call | tf_op jit(solution)/shard_map/swap_round/pallas_call | solution.py:364
  38.9 1.6 %hand_over.1 = (f32[8,4096]{1,0:T(8,128)}, f32[8,8,128]{2,1,0:T(8,128)}) custom-call(f32[8,4096]{1,0:T(8,128)} %get-tuple-element.4.panel_ref, f32[8,8,128]{2,1,0:T(8,128)} %bitcast.3), custom_call_target="tpu_custom_call" | custom-call | tf_op jit(solution)/shard_map/hand_over/pallas_call | solution.py:408
